TPU v7x, 256 devices: a whole 4x4x8 slice. The times are simulated.
256 devices in a mesh: depth: 4 (over z_hi), row: 4 (over x), col: 16 (over z_lo, y, core).
Axes of the slice: x: 4, y: 4, z: 8 (z_hi: 4, z_lo: 2; z = z_hi * 2 + z_lo), core: 2. Of those that a mesh axis runs over, the one named last changes fastest.
Arguments:
- activations: bfloat16 [2048, 12288], P(('depth', 'col'), 'row'), may hold values from -0.625 to 0.625
- out_grad: bfloat16 [2048, 18432], P(('depth', 'row'), 'col'), may hold values from -6 to 6
- weight: bfloat16 [12288, 18432], P('row', 'col'), may hold values from -0.078125 to 0.078125
Outputs:
- input_grad: bfloat16 [2048, 12288], P('depth', ('row', 'col'))
- weight_grad: float32 [4, 4, 768, 18432], P('row', 'depth', None, 'col')
All inputs are finite; a program needn't handle non-finite values.
Results may differ from a plain program's by a relative error of at most 0.001.
Values may be sent and summed in bfloat16 or wider, within the bound.
A program may use at most 128 MiB of HBM per device.

v0:
```python
import jax
import jax.numpy as jnp
from jax import lax
from jax.sharding import PartitionSpec as P


def body(activations, out_grad, weight):
    depth_rows = weight.shape[0] // lax.axis_size("depth")
    groups = lax.axis_size("depth")
    columns = lax.axis_size("col")
    split_part = lax.all_to_all(activations, "depth", split_axis=1, concat_axis=0, tiled=True)
    spread = lax.all_gather(split_part, "col", axis=0, tiled=True)
    everyone = lax.all_gather(out_grad, ("depth", "row"), axis=0, tiled=True)
    group_rows = everyone.shape[0] // groups
    short_rows = group_rows // columns
    weight_grad = jnp.einsum(
        "cgsa,gcsf->af",
        spread.reshape(columns, groups, short_rows, -1),
        everyone.reshape(groups, columns, short_rows, -1),
        preferred_element_type=jnp.float32,
    )
    grad_rows = lax.dynamic_slice_in_dim(
        everyone, lax.axis_index("depth") * group_rows, group_rows, 0
    )
    summed = lax.psum_scatter(
        lax.dot_general(
            weight, grad_rows, (((1,), (1,)), ((), ())), preferred_element_type=jnp.float32
        ),
        "col",
        scatter_dimension=0,
        tiled=True,
    )
    input_grad = summed.T.astype(jnp.bfloat16)
    return (input_grad, weight_grad.reshape(1, 1, depth_rows, -1))


def solution(mesh):
    placed = (P(("depth", "col"), "row"), P(("depth", "row"), "col"), P("row", "col"))
    return jax.shard_map(
        body,
        mesh=mesh,
        in_specs=placed,
        out_specs=(P("depth", ("row", "col")), P("row", "depth", None, "col")),
        check_vma=False,
    )
```

profile of v0, /device:TPU:1, one launch (start us, length us, event | category | flops | bytes accessed | tf_op | source)
XLA Modules:
  0.0 216.1 jit_solution(2802664829831302775)
XLA Ops:
  7.2 0.0 all-gather.3.cloned.1.call-start
  7.2 0.7 all-gather.3.cloned.1.call-update
  7.9 0.0 all-gather.5.cloned.1.call-start
  7.9 0.9 copy.24
  8.9 16.9 %all_to_all.19 = bf16[32,4,768]{2,0,1:T(8,128)(2,1)} all-to-all(bf16[32,4,768]{2,0,1:T(8,128)(2,1)S(1)} %bitcast.25), channel_id=1, replica_groups=mesh['depth'=4,'row'=4,'col'=16] {'depth'}, dimensions={1} | all-to-all | bytes 393216 | tf_op jit(solution)/shard_map/all_to_all | solution.py:11
  25.8 0.0 all-gather.5.cloned.1.call-update
  25.8 0.0 reduce-scatter.4.cloned.1.call-start
  25.9 71.0 %all-gather.3.cloned.1.call-done = bf16[2048,1152]{1,0:T(8,128)(2,1)} async-done(((bf16[128,1152]{1,0:T(8,128)(2,1)}), bf16[2048,1152]{1,0:T(8,128)(2,1)}) %all-gather.3.cloned.1.call-update) | async-done | bytes 4718608 | tf_op jit(solution)/shard_map/all_gather | solution.py:13
  96.9 10.3 %convolution_bitcast_fusion = f32[3072,512]{0,1:T(8,128)} fusion(bf16[3072,1152]{1,0:T(8,128)(2,1)} %param.5, bf16[2048,1152]{1,0:T(8,128)(2,1)} %all-gather.3.cloned.1.call-done, s32[]{:T(128)S(6)} %select_n.3), kind=kOutput, calls=%fused_computation | convolution fusion | flops 3623878656 | bytes 14548996 | tf_op jit(solution)/shard_map/dot_general | solution.py:26
  107.2 6.6 %copy.16 = f32[3072,512]{1,0:T(8,128)} copy(f32[3072,512]{0,1:T(8,128)} %convolution_bitcast_fusion) | data formatting | bytes 12582912
  113.8 0.0 reduce-scatter.4.cloned.1.call-update
  113.8 21.9 %all-gather.5.cloned.1.call-done = bf16[2048,768]{1,0:T(8,128)(2,1)} async-done(((bf16[128,768]{1,0:T(8,128)(2,1)}), bf16[2048,768]{1,0:T(8,128)(2,1)}) %all-gather.5.cloned.1.call-update) | async-done | bytes 3145744 | tf_op jit(solution)/shard_map/all_gather | solution.py:12
  135.7 9.4 %fusion.2 = f32[1,1,768,1152]{3,2,1,0:T(8,128)} fusion(bf16[16,4,32,768]{3,2,1,0:T(8,128)(2,1)} %bitcast.28, bf16[4,16,32,1152]{3,2,1,0:T(8,128)(2,1)} %bitcast.27), kind=kOutput, calls=%fused_computation.3 | convolution fusion | flops 3623878656 | bytes 11403264 | tf_op jit(solution)/shard_map/cgsa,gcsf->af/dot_general | solution.py:16
  145.1 62.6 %reduce-scatter.4.cloned.1.call-done = f32[192,512]{1,0:T(8,128)} async-done(((f32[3072,512]{1,0:T(8,128)}), f32[192,512]{1,0:T(8,128)}) %reduce-scatter.4.cloned.1.call-update) | async-done | bytes 393232
  207.7 1.1 copy.17
  208.8 0.8 copy.14
Async XLA Ops:
  7.2 89.7 %all-gather.3.cloned.1.call-start = ((), (), s32[]{:S(2)}) async-start(), calls=%async_computation.2 | async-start | bytes 5013504 | tf_op jit(solution)/shard_map/all_gather | solution.py:13
  7.9 127.8 %all-gather.5.cloned.1.call-start = ((), (), s32[]{:S(2)}) async-start(), calls=%async_computation.3 | async-start | bytes 3342336 | tf_op jit(solution)/shard_map/all_gather | solution.py:12
  25.8 181.8 %reduce-scatter.4.cloned.1.call-start = ((), (), s32[]{:S(2)}) async-start(), calls=%async_computation.4 | async-start | bytes 6684672
Sparse Core Ops, SparseCore 0:
  10.4 86.4 all-gather.2
  98.7 36.9 all-gather.4
  138.3 69.3 reduce-scatter.3
where the time goes:
time: 219 us; the launch traced here: 216 us
  waiting for transfers between devices  156 us (71%)
  matrix products  19.7 us (9%)
  blocking collectives  16.9 us (8%)
  between operations  13.8 us (6%)
  local copies, waits for them, and re-layouts  9.45 us (4%)
    all_gather x1, waiting for transfers between devices, body(): everyone = lax.all_gather(out_grad, ('depth', 'row'), axis=0, tiled=True)  71 us
    unnamed x4, waiting for transfers between devices  63.3 us
    all_gather x1, waiting for transfers between devices, body(): spread = lax.all_gather(split_part, 'col', axis=0, tiled=True)  21.9 us
    all_to_all x1, blocking collectives, body(): lax.all_to_all(activations, 'depth', split_axis=1, concat_axis=0, tiled=T...  16.9 us
    dot_general x1, matrix products, body(): lax.dot_general(weight, grad_rows, (((1,), (1,)), ((), ())), preferred_el...  10.3 us
    dot_general x1, matrix products, body(): jnp.einsum('cgsa,gcsf->af', spread.reshape(columns, groups, short_rows, -...  9.38 us
    unnamed x3, local copies, waits for them, and re-layouts  8.51 us
  transfers between devices with their start and end apart: 3, of which 3 were waited for; matrix products, arithmetic and copies ran while one was open for 13% of the time, Pallas kernels for 0%

commit v1 on v0

v1 whole, which is shorter than its diff:
```python
import jax
import jax.numpy as jnp
from jax import lax
from jax.experimental import pallas as pl
from jax.experimental.pallas import tpu as pltpu
from jax.sharding import PartitionSpec as P

F32 = jnp.float32
BF16 = jnp.bfloat16
SEMS = 112


def kernel(act, og, wt, ig_out, wg_out, W, OG, OGP, ACT, PT, R1, R2, SZ, RZ, FN, ACC, ssem, rsem, lsem):
    h = lax.axis_index("depth")
    x = lax.axis_index("row")
    c = lax.axis_index("col")
    k = lax.rem(c, 2)
    y = lax.rem(lax.div(c, 2), 4)
    l = lax.div(c, 8)
    ok, ol = 1 - k, 1 - l
    up = lambda v: lax.rem(v + 1, 4)
    dn = lambda v: lax.rem(v + 3, 4)
    op = lambda v: lax.rem(v + 2, 4)
    xp, xm, x2 = up(x), dn(x), op(x)
    yp, ym, y2 = up(y), dn(y), op(y)
    hp, hm, h2 = up(h), dn(h), op(h)
    col = lambda l_, y_, k_: (l_ * 4 + y_) * 2 + k_
    to_xp, to_xm = {"row": xp}, {"row": xm}
    to_hp, to_hm = {"depth": hp}, {"depth": hm}
    to_yp, to_ym = {"col": col(l, yp, k)}, {"col": col(l, ym, k)}
    to_core, to_pair = {"col": col(l, y, ok)}, {"col": col(ol, y, k)}
    plane = [to_hp, to_hm, {"depth": h2}, to_pair] + [
        {"depth": d, "col": col(ol, y, k)} for d in (hp, hm, h2)
    ]

    barrier = pltpu.get_barrier_semaphore()
    greeted = plane + [to_xp, to_xm, to_yp, to_ym, to_core]
    for dev in greeted:
        pl.semaphore_signal(barrier, inc=1, device_id=dev, device_id_type=pl.DeviceIdType.MESH)

    started = []

    def send(src, dst, dev):
        i = len(started)
        d = pltpu.make_async_remote_copy(
            src_ref=src, dst_ref=dst, send_sem=ssem.at[i], recv_sem=rsem.at[i],
            device_id=dev, device_id_type=pl.DeviceIdType.MESH,
        )
        d.start()
        started.append(d)
        return d

    locs = []

    def local(src, dst):
        d = pltpu.make_async_copy(src, dst, lsem.at[len(locs)])
        d.start()
        locs.append(d)
        return d

    HA, HB = pl.ds(0, 64), pl.ds(64, 64)
    cols_of = lambda d: pl.ds(pl.multiple_of(d * 768, 768), 768)

    l_og = local(og, OG.at[h, x])
    l_w = local(wt.at[:, :, k], W.at[:, :, :, pl.ds(0, 1152)])
    l_act = local(act.at[:, cols_of(h)], ACT.at[h, l, y, k])
    pl.semaphore_wait(barrier, len(greeted))

    mine = lambda half: og.at[half]
    d_core_og = [send(og, OGP.at[0], to_core)]
    x0a = send(mine(HA), OG.at[h, x, HA], to_xp)
    x0b = send(mine(HB), OG.at[h, x, HB], to_xm)
    z0a = send(mine(HA), OG.at[h, x, HA], to_hp)
    z0b = send(mine(HB), OG.at[h, x, HB], to_hm)
    d_w = send(wt.at[:, :, ok], W.at[:, :, :, pl.ds(1152, 1152)], to_core)
    x0c = send(mine(HB), OG.at[h, x, HB], to_xp)
    x0d = send(mine(HA), OG.at[h, x, HA], to_xm)
    d_act = []
    for dev in plane:
        d_act.append(send(act.at[:, cols_of(dev.get("depth", h))], ACT.at[h, l, y, k], dev))
    z0c = send(mine(HB), OG.at[h, x, HB], to_hp)
    z0d = send(mine(HA), OG.at[h, x, HA], to_hm)

    def fwd_x(H, first, second):
        first.wait_recv()
        f0 = send(OG.at[H, xm, HA], OG.at[H, xm, HA], to_xp)
        second.wait_recv()
        f1 = send(OG.at[H, xp, HB], OG.at[H, xp, HB], to_xm)
        return f0, f1

    order = [x, xm, xp, x2]

    def part(t):
        ogs = jnp.concatenate([OG[h, order[t]], OGP[t]], axis=1)

        @pl.loop(0, 2)
        def _(i):
            w = W[i].reshape(768, 2304)
            PT[t, i] = lax.dot_general(
                w, ogs, (((1,), (1,)), ((), ())), preferred_element_type=F32
            ).reshape(4, 192, 128)

    FA, FB = pl.ds(0, 96), pl.ds(96, 96)

    def rs_begin(t):
        part(t)
        return dict(
            p1=send(PT.at[t, :, y2, FA], R1.at[t, 0], to_yp),
            m1=send(PT.at[t, :, y2, FB], R1.at[t, 1], to_ym),
            p2=send(PT.at[t, :, yp, FB], R2.at[t, 0, :, FB], to_yp),
            m2=send(PT.at[t, :, ym, FA], R2.at[t, 1, :, FA], to_ym),
        )

    def rs_mid(t, s):
        s["p1"].wait_recv()
        PT[t, :, yp, FA] = PT[t, :, yp, FA] + R1[t, 0]
        s["p3"] = send(PT.at[t, :, yp, FA], R2.at[t, 0, :, FA], to_yp)
        s["m1"].wait_recv()
        PT[t, :, ym, FB] = PT[t, :, ym, FB] + R1[t, 1]
        s["m3"] = send(PT.at[t, :, ym, FB], R2.at[t, 1, :, FB], to_ym)

    def rs_end(t, s):
        for n in ("p2", "m2", "p3", "m3"):
            s[n].wait_recv()
        SZ[t] = PT[t, ol, y] + R2[t, 0, ol] + R2[t, 1, ol]
        s["z"] = send(SZ.at[t], RZ.at[t], to_pair)
        FN[t] = PT[t, l, y] + R2[t, 0, l] + R2[t, 1, l]

    def rs_out(t, s):
        s["z"].wait_recv()
        FN[t] = FN[t] + RZ[t]
        return local(FN.at[t], ig_out.at[order[t]])

    def wg(H, first, last):
        for m in range(3):
            rows = pl.ds(m * 256, 256)
            a = ACT[H, :, :, :, :, rows].reshape(512, 256)
            g = OG[H].reshape(512, 1152)
            d = lax.dot_general(a, g, (((0,), (0,)), ((), ())), preferred_element_type=F32)
            ACC[rows] = d if first else ACC[rows] + d
            if last:
                local(ACC.at[rows], wg_out.at[rows])

    l_og.wait()
    x0e, x0f = fwd_x(h, x0a, x0b)
    x0c.wait_recv()
    d_core_og.append(send(OG.at[h, xm], OGP.at[1], to_core))
    x0d.wait_recv()
    d_core_og.append(send(OG.at[h, xp], OGP.at[2], to_core))
    l_w.wait()
    d_w.wait_recv()
    d_core_og[0].wait_recv()
    s0 = rs_begin(0)

    z0a.wait_recv()
    a1 = send(OG.at[hm, x, HA], OG.at[hm, x, HA], to_xp)
    z2a = send(OG.at[hm, x, HA], OG.at[hm, x, HA], to_hp)
    a2 = send(OG.at[hm, x, HA], OG.at[hm, x, HA], to_xm)
    z0b.wait_recv()
    b1 = send(OG.at[hp, x, HB], OG.at[hp, x, HB], to_xm)
    z2b = send(OG.at[hp, x, HB], OG.at[hp, x, HB], to_hm)
    b2 = send(OG.at[hp, x, HB], OG.at[hp, x, HB], to_xp)

    for d in d_act:
        d.wait_recv()
    l_act.wait()
    y_p = send(ACT.at[:, :, y, k], ACT.at[:, :, y, k], to_yp)
    y_m = send(ACT.at[:, :, y, k], ACT.at[:, :, y, k], to_ym)
    c_act = [send(ACT.at[:, :, y, k], ACT.at[:, :, y, k], to_core)]

    x0e.wait_recv()
    x0f.wait_recv()
    d_core_og.append(send(OG.at[h, x2], OGP.at[3], to_core))
    d_core_og[1].wait_recv()
    s1 = rs_begin(1)
    rs_mid(0, s0)
    d_core_og[2].wait_recv()
    s2 = rs_begin(2)

    z0c.wait_recv()
    a3 = send(OG.at[hm, x, HB], OG.at[hm, x, HB], to_xm)
    a4 = send(OG.at[hm, x, HB], OG.at[hm, x, HB], to_xp)
    z0d.wait_recv()
    b3 = send(OG.at[hp, x, HA], OG.at[hp, x, HA], to_xp)
    b4 = send(OG.at[hp, x, HA], OG.at[hp, x, HA], to_xm)

    d_core_og[3].wait_recv()
    s3 = rs_begin(3)
    rs_mid(1, s1)
    rs_end(0, s0)
    a5, a6 = fwd_x(hm, a1, a3)
    b5, b6 = fwd_x(hp, b3, b1)

    y_p.wait_recv()
    y_fp = send(ACT.at[:, 0, ym, k], ACT.at[:, 0, ym, k], to_yp)
    c_act.append(send(ACT.at[:, :, ym, k], ACT.at[:, :, ym, k], to_core))
    y_m.wait_recv()
    y_fm = send(ACT.at[:, 1, yp, k], ACT.at[:, 1, yp, k], to_ym)
    c_act.append(send(ACT.at[:, :, yp, k], ACT.at[:, :, yp, k], to_core))

    z2a.wait_recv()
    e1 = send(OG.at[h2, x, HA], OG.at[h2, x, HA], to_xp)
    e2 = send(OG.at[h2, x, HA], OG.at[h2, x, HA], to_xm)
    z2b.wait_recv()
    e3 = send(OG.at[h2, x, HB], OG.at[h2, x, HB], to_xm)
    e4 = send(OG.at[h2, x, HB], OG.at[h2, x, HB], to_xp)

    rs_mid(2, s2)
    rs_mid(3, s3)
    rs_end(1, s1)
    y_fp.wait_recv()
    y_fm.wait_recv()
    c_act.append(send(ACT.at[:, :, y2, k], ACT.at[:, :, y2, k], to_core))
    rs_out(0, s0)
    e5, e6 = fwd_x(h2, e1, e3)
    rs_end(2, s2)
    rs_out(1, s1)
    for d in c_act:
        d.wait_recv()
    wg(h, True, False)
    for d in (a2, a4, a5, a6):
        d.wait_recv()
    for d in (b2, b4, b5, b6):
        d.wait_recv()
    rs_end(3, s3)
    rs_out(2, s2)
    wg(hm, False, False)
    wg(hp, False, False)
    rs_out(3, s3)
    for d in (e2, e4, e5, e6):
        d.wait_recv()
    wg(h2, False, True)
    for d in locs[3:]:
        d.wait()
    for d in started:
        d.wait_send()


def body(activations, out_grad, weight):
    any_ = pl.BlockSpec(memory_space=pl.ANY)
    ig, wg = pl.pallas_call(
        kernel,
        out_shape=(
            jax.ShapeDtypeStruct((4, 192, 128), F32),
            jax.ShapeDtypeStruct((768, 1152), F32),
        ),
        in_specs=[any_] * 3,
        out_specs=(any_, any_),
        scratch_shapes=[
            pltpu.VMEM((2, 4, 192, 2304), BF16),
            pltpu.VMEM((4, 4, 128, 1152), BF16),
            pltpu.VMEM((4, 128, 1152), BF16),
            pltpu.VMEM((4, 2, 4, 2, 32, 768), BF16),
            pltpu.VMEM((4, 2, 4, 192, 128), F32),
            pltpu.VMEM((4, 2, 2, 96, 128), F32),
            pltpu.VMEM((4, 2, 2, 192, 128), F32),
            pltpu.VMEM((4, 192, 128), F32),
            pltpu.VMEM((4, 192, 128), F32),
            pltpu.VMEM((4, 192, 128), F32),
            pltpu.VMEM((768, 1152), F32),
            pltpu.SemaphoreType.DMA((SEMS,)),
            pltpu.SemaphoreType.DMA((SEMS,)),
            pltpu.SemaphoreType.DMA((16,)),
        ],
        compiler_params=pltpu.CompilerParams(
            collective_id=0, has_side_effects=True, vmem_limit_bytes=56 * 1024 * 1024
        ),
        cost_estimate=pl.CostEstimate(flops=7_300_000_000, bytes_accessed=20_000_000, transcendentals=0),
    )(activations, out_grad, weight.reshape(2, 4, 2, 192, 1152))
    input_grad = jnp.transpose(ig, (0, 2, 1)).reshape(512, 192).astype(BF16)
    return input_grad, wg.reshape(1, 1, 768, 1152)


def solution(mesh):
    return jax.shard_map(
        body,
        mesh=mesh,
        in_specs=(P(("depth", "col"), "row"), P(("depth", "row"), "col"), P("row", "col")),
        out_specs=(P("depth", ("row", "col")), P("row", "depth", None, "col")),
        check_vma=False,
    )
```

time: 219 us -> 77.9 us (0.36); the launches traced: 216 us -> 77.8 us
  waiting for transfers between devices: 156 us -> 0 us
  Pallas kernels: 0 us -> 71.4 us
  matrix products: 19.7 us -> 0 us
  blocking collectives: 16.9 us -> 0 us
  between operations: 13.8 us -> 0.64 us
  local copies, waits for them, and re-layouts: 9.45 us -> 4.02 us
    all_gather x2 -> x0, waiting for transfers between devices: 92.9 us -> none  [the longest x1 71 us: body(): everyone = lax.all_gather(out_grad, ('depth', 'row'), axis=0, tiled=True)]
    pallas_call x0 -> x1, Pallas kernels: none -> 71.4 us  [body(): pl.pallas_call(kernel, out_shape=(jax.ShapeDtypeStruct((4, 192, 128), F32...]
    unnamed x4 -> x0, waiting for transfers between devices: 63.3 us -> none
    dot_general x2 -> x0, matrix products: 19.7 us -> none  [the longest x1 10.3 us: body(): lax.dot_general(weight, grad_rows, (((1,), (1,)), ((), ())), preferred_el...]
    all_to_all x1 -> x0, blocking collectives: 16.9 us -> none  [body(): lax.all_to_all(activations, 'depth', split_axis=1, concat_axis=0, tiled=T...]
    unnamed x3 -> x1, local copies, waits for them, and re-layouts: 8.51 us -> 4.02 us
  transfers between devices with their start and end apart: 3 -> 0, of which waited for: 3 -> 0; matrix products, arithmetic and copies ran while one was open for 13% -> 0% of each run, Pallas kernels for 0% -> 0%
where the time goes in v1:
time: 77.9 us; the launch traced here: 77.8 us
  Pallas kernels  71.4 us (92%)
  local copies, waits for them, and re-layouts  4.02 us (5%)
  other arithmetic  1.69 us (2%)
    pallas_call x1, Pallas kernels, body(): pl.pallas_call(kernel, out_shape=(jax.ShapeDtypeStruct((4, 192, 128), F32...  71.4 us
    unnamed x1, local copies, waits for them, and re-layouts  4.02 us
    convert_element_type x1, other arithmetic, body(): input_grad = jnp.transpose(ig, (0, 2, 1)).reshape(512, 192).astype(BF16)  1.69 us

profile of v1, /device:TPU:1, one launch (start us, length us, event | category | flops | bytes accessed | tf_op | source)
XLA Modules:
  0.0 77.8 jit_solution(2456369208495841812)
XLA Ops:
  0.6 71.4 %shard_map.50 = (f32[4,192,128]{2,1,0:T(8,128)}, f32[768,1152]{1,0:T(8,128)}) custom-call(bf16[32,3072]{1,0:T(8,128)(2,1)} %act.1, bf16[128,1152]{1,0:T(8,128)(2,1)} %og.1, bf16[2,4,2,192,1152]{4,3,2,1,0:T(8,128)(2,1)} %bitcast.9), custom_call_target="tpu_custom_call" | custom-call | flops 7299999744 | bytes 20000000 | tf_op jit(solution)/shard_map/pallas_call | solution.py:241
  72.0 1.7 %copy_bitcast_fusion = bf16[512,192]{0,1:T(8,128)(2,1)} fusion(f32[4,192,128]{2,1,0:T(8,128)} %get-tuple-element.4), kind=kLoop, calls=%fused_computation | loop fusion | flops 98304 | bytes 589824 | tf_op jit(solution)/shard_map/convert_element_type | solution.py:270
  73.7 4.0 %copy.9 = f32[1,1,768,1152]{3,2,1,0:T(8,128)} copy(f32[1,1,768,1152]{3,2,1,0:T(8,128)} %bitcast.8) | data formatting | bytes 7077888

commit v2 on v0

v2 whole, which is shorter than its diff:
```python
import jax
import jax.numpy as jnp
from jax import lax
from jax.experimental import pallas as pl
from jax.experimental.pallas import tpu as pltpu
from jax.sharding import PartitionSpec as P

F32 = jnp.float32
BF16 = jnp.bfloat16
SEMS = 64


def kernel(act, og, wt, ig_out, wg_out, W, OG, OGP, ACT, PT, R1, R2, SZ, RZ, FN, ACC, ssem, rsem, lsem):
    h = lax.axis_index("depth")
    x = lax.axis_index("row")
    c = lax.axis_index("col")
    k = lax.rem(c, 2)
    y = lax.rem(lax.div(c, 2), 4)
    l = lax.div(c, 8)
    ok, ol = 1 - k, 1 - l
    up = lambda v: lax.rem(v + 1, 4)
    dn = lambda v: lax.rem(v + 3, 4)
    op = lambda v: lax.rem(v + 2, 4)
    xp, xm, x2 = up(x), dn(x), op(x)
    yp, ym, y2 = up(y), dn(y), op(y)
    hp, hm, h2 = up(h), dn(h), op(h)
    col = lambda l_, y_, k_: (l_ * 4 + y_) * 2 + k_
    to_xp, to_xm = {"row": xp}, {"row": xm}
    to_hp, to_hm = {"depth": hp}, {"depth": hm}
    to_yp, to_ym = {"col": col(l, yp, k)}, {"col": col(l, ym, k)}
    to_core, to_pair = {"col": col(l, y, ok)}, {"col": col(ol, y, k)}
    plane = [to_hp, to_hm, {"depth": h2}, to_pair] + [
        {"depth": d, "col": col(ol, y, k)} for d in (hp, hm, h2)
    ]

    barrier = pltpu.get_barrier_semaphore()
    greeted = plane + [to_xp, to_xm, to_yp, to_ym, to_core]
    for dev in greeted:
        pl.semaphore_signal(barrier, inc=1, device_id=dev, device_id_type=pl.DeviceIdType.MESH)

    started = []
    used = [0]

    class Group:
        def __init__(self, whole):
            self.i = used[0]
            used[0] += 1
            self.d = pltpu.make_async_remote_copy(
                src_ref=whole, dst_ref=whole, send_sem=ssem.at[self.i], recv_sem=rsem.at[self.i],
                device_id=to_core, device_id_type=pl.DeviceIdType.MESH,
            )
            started.append(self.d)

        def send(self, src, dst, dev):
            pltpu.make_async_remote_copy(
                src_ref=src, dst_ref=dst, send_sem=ssem.at[self.i], recv_sem=rsem.at[self.i],
                device_id=dev, device_id_type=pl.DeviceIdType.MESH,
            ).start()

        def wait(self):
            self.d.wait_recv()

    def send(src, dst, dev):
        g = Group(dst)
        g.send(src, dst, dev)
        return g

    locs = []

    def local(src, dst):
        d = pltpu.make_async_copy(src, dst, lsem.at[len(locs)])
        d.start()
        locs.append(d)
        return d

    HA, HB = pl.ds(0, 64), pl.ds(64, 64)
    cols_of = lambda d: pl.ds(pl.multiple_of(d * 768, 768), 768)

    l_og = local(og, OG.at[h, x])
    l_w = local(wt.at[:, :, k], W.at[:, :, :, pl.ds(0, 1152)])
    l_act = local(act.at[:, cols_of(h)], ACT.at[h, l, y, k])
    pl.semaphore_wait(barrier, len(greeted))

    two_halves = OG.at[h, x]
    depths = [h, hm, hp, h2]

    x0a = send(og.at[HA], OG.at[h, x, HA], to_xp)
    x0b = send(og.at[HB], OG.at[h, x, HB], to_xm)
    z0ab, z0cd, z2ab = Group(two_halves), Group(two_halves), Group(two_halves)
    z0ab.send(og.at[HA], OG.at[h, x, HA], to_hp)
    z0ab.send(og.at[HB], OG.at[h, x, HB], to_hm)
    c_og0 = send(og, OGP.at[0], to_core)
    ring = [y2, yp, ym, y]
    to_other = lambda v: send(wt.at[:, v, ok], W.at[:, v, :, pl.ds(1152, 1152)], to_core)
    d_w = [to_other(v) for v in ring[:2]]
    x0cd, x0ef = Group(two_halves), Group(two_halves)
    x0cd.send(og.at[HB], OG.at[h, x, HB], to_xp)
    x0cd.send(og.at[HA], OG.at[h, x, HA], to_xm)
    y_pm = [Group(ACT.at[d, :, pl.ds(0, 2), k]) for d in depths]
    own_act = act.at[:, cols_of(h)]
    y_pm[0].send(own_act, ACT.at[h, l, y, k], to_yp)
    y_pm[0].send(own_act, ACT.at[h, l, y, k], to_ym)
    d_w += [to_other(v) for v in ring[2:]]
    z0cd.send(og.at[HB], OG.at[h, x, HB], to_hp)
    z0cd.send(og.at[HA], OG.at[h, x, HA], to_hm)
    d_act = []
    for dev in plane:
        d_act.append(send(act.at[:, cols_of(dev.get("depth", h))], ACT.at[h, l, y, k], dev))

    order = [x, xm, xp, x2]
    FA, FB = pl.ds(0, 96), pl.ds(96, 96)

    class Terms:
        def __init__(self, t, n):
            self.t, self.n, self.at = t, n, pl.ds(t, n)
            self.g1, self.g2 = Group(R1.at[self.at]), Group(R2.at[self.at])

        def load(self):
            own = [OG[h, order[t]] for t in range(self.t, self.t + self.n)]
            other = [OGP[t] for t in range(self.t, self.t + self.n)]
            self.ogs = jnp.concatenate(
                [jnp.concatenate(own, axis=0), jnp.concatenate(other, axis=0)], axis=1
            )

        def part(self, i):
            v = ring[i]
            r = lax.dot_general(
                W[:, v].reshape(384, 2304), self.ogs, (((1,), (1,)), ((), ())),
                preferred_element_type=F32,
            )
            for j in range(self.n):
                PT[self.t + j, :, v] = r[:, j * 128 : (j + 1) * 128].reshape(2, 192, 128)

        def far(self):
            self.part(0)
            self.g1.send(PT.at[self.at, :, y2, FA], R1.at[self.at, 0], to_yp)
            self.g1.send(PT.at[self.at, :, y2, FB], R1.at[self.at, 1], to_ym)

        def near_p(self):
            self.part(1)
            self.g2.send(PT.at[self.at, :, yp, FB], R2.at[self.at, 0, :, FB], to_yp)

        def near_m(self):
            self.part(2)
            self.g2.send(PT.at[self.at, :, ym, FA], R2.at[self.at, 1, :, FA], to_ym)

        def all(self):
            self.load()
            self.far()
            self.near_p()
            self.near_m()
            self.part(3)

        def mid(self):
            self.g1.wait()
            for t in range(self.t, self.t + self.n):
                PT[t, :, yp, FA] = PT[t, :, yp, FA] + R1[t, 0]
                PT[t, :, ym, FB] = PT[t, :, ym, FB] + R1[t, 1]
            self.g2.send(PT.at[self.at, :, yp, FA], R2.at[self.at, 0, :, FA], to_yp)
            self.g2.send(PT.at[self.at, :, ym, FB], R2.at[self.at, 1, :, FB], to_ym)

        def end(self):
            self.g2.wait()
            for t in range(self.t, self.t + self.n):
                SZ[t] = PT[t, ol, y] + R2[t, 0, ol] + R2[t, 1, ol]
            self.z = send(SZ.at[self.at], RZ.at[self.at], to_pair)
            for t in range(self.t, self.t + self.n):
                FN[t] = PT[t, l, y] + R2[t, 0, l] + R2[t, 1, l]

        def out(self):
            self.z.wait()
            for t in range(self.t, self.t + self.n):
                FN[t] = FN[t] + RZ[t]
                local(FN.at[t], ig_out.at[order[t]])

    def wg(H, first, last):
        for m in range(3):
            rows = pl.ds(m * 256, 256)
            a = ACT[H, :, :, :, :, rows].reshape(512, 256)
            g = OG[H].reshape(512, 1152)
            d = lax.dot_general(a, g, (((0,), (0,)), ((), ())), preferred_element_type=F32)
            ACC[rows] = d if first else ACC[rows] + d
            if last:
                local(ACC.at[rows], wg_out.at[rows])

    def again(group, H, X, half, dev):
        group.send(OG.at[H, X, half], OG.at[H, X, half], dev)

    s0, s1, s3 = Terms(0, 1), Terms(1, 2), Terms(3, 1)
    l_og.wait()
    l_w.wait()
    c_og0.wait()
    s0.load()
    d_w[0].wait()
    s0.far()
    d_w[1].wait()
    s0.near_p()
    x0a.wait()
    again(x0ef, h, xm, HA, to_xp)
    x0b.wait()
    again(x0ef, h, xp, HB, to_xm)
    d_w[2].wait()
    s0.near_m()
    d_w[3].wait()
    s0.part(3)
    s0.mid()
    c_og12 = Group(OGP.at[pl.ds(1, 2)])
    x0cd.wait()
    c_og12.send(OG.at[h, xm], OGP.at[1], to_core)
    c_og12.send(OG.at[h, xp], OGP.at[2], to_core)

    ab1, ab3 = Group(two_halves), Group(two_halves)
    a_in, b_in = Group(OG.at[h, pl.ds(0, 2)]), Group(OG.at[h, pl.ds(0, 2)])
    z0ab.wait()
    again(ab1, hm, x, HA, to_xp)
    again(ab1, hp, x, HB, to_xm)
    again(a_in, hm, x, HA, to_xm)
    again(b_in, hp, x, HB, to_xp)
    again(z2ab, hm, x, HA, to_hp)
    again(z2ab, hp, x, HB, to_hm)

    c_og12.wait()
    s1.all()
    x0ef.wait()
    c_og3 = send(OG.at[h, x2], OGP.at[3], to_core)
    s0.end()
    c_og3.wait()
    s3.all()
    ab1.wait()
    again(a_in, hm, xm, HA, to_xp)
    again(b_in, hp, xp, HB, to_xm)
    s1.mid()
    z0cd.wait()
    again(ab3, hm, x, HB, to_xm)
    again(ab3, hp, x, HA, to_xp)
    again(a_in, hm, x, HB, to_xp)
    again(b_in, hp, x, HA, to_xm)
    s3.mid()

    def act_y(i):
        d = depths[i]
        own = ACT.at[d, ol, y, k] if i == 0 else ACT.at[d, :, y, k]
        y_pm[i].send(own, own, to_yp)
        y_pm[i].send(own, own, to_ym)

    y_f = [Group(ACT.at[d, :, 0, k]) for d in depths]
    c_act = [Group(ACT.at[d, :, pl.ds(0, 3), k]) for d in depths]

    def act_in(i):
        d = depths[i]
        y_pm[i].wait()
        y_f[i].send(ACT.at[d, 0, ym, k], ACT.at[d, 0, ym, k], to_yp)
        y_f[i].send(ACT.at[d, 1, yp, k], ACT.at[d, 1, yp, k], to_ym)
        for v in (ym, yp):
            c_act[i].send(ACT.at[d, :, v, k], ACT.at[d, :, v, k], to_core)

    def act_all(i):
        d = depths[i]
        y_f[i].wait()
        c_act[i].send(ACT.at[d, :, y2, k], ACT.at[d, :, y2, k], to_core)

    for d in d_act:
        d.wait()
    l_act.wait()
    act_y(0)
    act_y(1)
    c_own = send(ACT.at[:, :, y, k], ACT.at[:, :, y, k], to_core)
    ab3.wait()
    again(b_in, hp, xm, HA, to_xp)
    again(a_in, hm, xp, HB, to_xm)
    s0.out()
    s1.end()
    e13, e_in = Group(two_halves), Group(OG.at[h, pl.ds(0, 2)])
    z2ab.wait()
    again(e13, h2, x, HA, to_xp)
    again(e13, h2, x, HB, to_xm)
    again(e_in, h2, x, HA, to_xm)
    again(e_in, h2, x, HB, to_xp)
    s3.end()
    act_in(0)
    act_y(2)
    s1.out()
    act_in(1)
    act_y(3)
    act_all(0)
    s3.out()
    e13.wait()
    again(e_in, h2, xm, HA, to_xp)
    again(e_in, h2, xp, HB, to_xm)
    c_own.wait()
    c_act[0].wait()
    wg(h, True, False)
    act_in(2)
    act_all(1)
    a_in.wait()
    c_act[1].wait()
    wg(hm, False, False)
    act_in(3)
    act_all(2)
    b_in.wait()
    c_act[2].wait()
    wg(hp, False, False)
    act_all(3)
    e_in.wait()
    c_act[3].wait()
    wg(h2, False, True)
    for d in locs[3:]:
        d.wait()
    for d in started:
        d.wait_send()


def body(activations, out_grad, weight):
    any_ = pl.BlockSpec(memory_space=pl.ANY)
    ig, wg = pl.pallas_call(
        kernel,
        out_shape=(
            jax.ShapeDtypeStruct((4, 192, 128), F32),
            jax.ShapeDtypeStruct((768, 1152), F32),
        ),
        in_specs=[any_] * 3,
        out_specs=(any_, any_),
        scratch_shapes=[
            pltpu.VMEM((2, 4, 192, 2304), BF16),
            pltpu.VMEM((4, 4, 128, 1152), BF16),
            pltpu.VMEM((4, 128, 1152), BF16),
            pltpu.VMEM((4, 2, 4, 2, 32, 768), BF16),
            pltpu.VMEM((4, 2, 4, 192, 128), F32),
            pltpu.VMEM((4, 2, 2, 96, 128), F32),
            pltpu.VMEM((4, 2, 2, 192, 128), F32),
            pltpu.VMEM((4, 192, 128), F32),
            pltpu.VMEM((4, 192, 128), F32),
            pltpu.VMEM((4, 192, 128), F32),
            pltpu.VMEM((768, 1152), F32),
            pltpu.SemaphoreType.DMA((SEMS,)),
            pltpu.SemaphoreType.DMA((SEMS,)),
            pltpu.SemaphoreType.DMA((16,)),
        ],
        compiler_params=pltpu.CompilerParams(
            collective_id=0, has_side_effects=True, vmem_limit_bytes=56 * 1024 * 1024
        ),
        cost_estimate=pl.CostEstimate(flops=7_300_000_000, bytes_accessed=20_000_000, transcendentals=0),
    )(activations, out_grad, weight.reshape(2, 4, 2, 192, 1152))
    input_grad = jnp.transpose(ig, (0, 2, 1)).reshape(512, 192).astype(BF16)
    return input_grad, wg.reshape(1, 1, 768, 1152)


def solution(mesh):
    return jax.shard_map(
        body,
        mesh=mesh,
        in_specs=(P(("depth", "col"), "row"), P(("depth", "row"), "col"), P("row", "col")),
        out_specs=(P("depth", ("row", "col")), P("row", "depth", None, "col")),
        check_vma=False,
    )
```

time: 219 us -> 70.3 us (0.32); the launches traced: 216 us -> 70.1 us
  waiting for transfers between devices: 156 us -> 0 us
  Pallas kernels: 0 us -> 63.8 us
  matrix products: 19.7 us -> 0 us
  blocking collectives: 16.9 us -> 0 us
  between operations: 13.8 us -> 0.64 us
  local copies, waits for them, and re-layouts: 9.45 us -> 4.02 us
    all_gather x2 -> x0, waiting for transfers between devices: 92.9 us -> none  [the longest x1 71 us: body(): everyone = lax.all_gather(out_grad, ('depth', 'row'), axis=0, tiled=True)]
    pallas_call x0 -> x1, Pallas kernels: none -> 63.8 us  [body(): pl.pallas_call(kernel, out_shape=(jax.ShapeDtypeStruct((4, 192, 128), F32...]
    unnamed x4 -> x0, waiting for transfers between devices: 63.3 us -> none
    dot_general x2 -> x0, matrix products: 19.7 us -> none  [the longest x1 10.3 us: body(): lax.dot_general(weight, grad_rows, (((1,), (1,)), ((), ())), preferred_el...]
    all_to_all x1 -> x0, blocking collectives: 16.9 us -> none  [body(): lax.all_to_all(activations, 'depth', split_axis=1, concat_axis=0, tiled=T...]
    unnamed x3 -> x1, local copies, waits for them, and re-layouts: 8.51 us -> 4.02 us
  transfers between devices with their start and end apart: 3 -> 0, of which waited for: 3 -> 0; matrix products, arithmetic and copies ran while one was open for 13% -> 0% of each run, Pallas kernels for 0% -> 0%
where the time goes in v2:
time: 70.3 us; the launch traced here: 70.1 us
  Pallas kernels  63.8 us (91%)
  local copies, waits for them, and re-layouts  4.02 us (6%)
  other arithmetic  1.69 us (2%)
    pallas_call x1, Pallas kernels, body(): pl.pallas_call(kernel, out_shape=(jax.ShapeDtypeStruct((4, 192, 128), F32...  63.8 us
    unnamed x1, local copies, waits for them, and re-layouts  4.02 us
    convert_element_type x1, other arithmetic, body(): input_grad = jnp.transpose(ig, (0, 2, 1)).reshape(512, 192).astype(BF16)  1.69 us

profile of v2, /device:TPU:1, one launch (start us, length us, event | category | flops | bytes accessed | tf_op | source)
XLA Modules:
  0.0 70.1 jit_solution(11386719458715303441)
XLA Ops:
  0.6 63.8 %shard_map.50 = (f32[4,192,128]{2,1,0:T(8,128)}, f32[768,1152]{1,0:T(8,128)}) custom-call(bf16[32,3072]{1,0:T(8,128)(2,1)} %act.1, bf16[128,1152]{1,0:T(8,128)(2,1)} %og.1, bf16[2,4,2,192,1152]{4,3,2,1,0:T(8,128)(2,1)} %bitcast.9), custom_call_target="tpu_custom_call" | custom-call | flops 7299999744 | bytes 20000000 | tf_op jit(solution)/shard_map/pallas_call | solution.py:315
  64.4 1.7 %copy_bitcast_fusion = bf16[512,192]{0,1:T(8,128)(2,1)} fusion(f32[4,192,128]{2,1,0:T(8,128)} %get-tuple-element.4), kind=kLoop, calls=%fused_computation | loop fusion | flops 98304 | bytes 589824 | tf_op jit(solution)/shard_map/convert_element_type | solution.py:344
  66.1 4.0 %copy.9 = f32[1,1,768,1152]{3,2,1,0:T(8,128)} copy(f32[1,1,768,1152]{3,2,1,0:T(8,128)} %bitcast.8) | data formatting | bytes 7077888

commit v3 on v2

--- a/solution.py
+++ b/solution.py
@@ -10,7 +10,7 @@
 SEMS = 64
 
 
-def kernel(act, og, wt, ig_out, wg_out, W, OG, OGP, ACT, PT, R1, R2, SZ, RZ, FN, ACC, ssem, rsem, lsem):
+def kernel(act, og, wt, ig_out, ACC, W, OG, OGP, ACT, PT, R1, R2, SZ, RZ, FN, ssem, rsem, lsem):
     h = lax.axis_index("depth")
     x = lax.axis_index("row")
     c = lax.axis_index("col")
@@ -132,24 +132,23 @@
                 PT[self.t + j, :, v] = r[:, j * 128 : (j + 1) * 128].reshape(2, 192, 128)
 
         def far(self):
-            self.part(0)
             self.g1.send(PT.at[self.at, :, y2, FA], R1.at[self.at, 0], to_yp)
             self.g1.send(PT.at[self.at, :, y2, FB], R1.at[self.at, 1], to_ym)
 
-        def near_p(self):
-            self.part(1)
+        def near(self):
             self.g2.send(PT.at[self.at, :, yp, FB], R2.at[self.at, 0, :, FB], to_yp)
-
-        def near_m(self):
-            self.part(2)
             self.g2.send(PT.at[self.at, :, ym, FA], R2.at[self.at, 1, :, FA], to_ym)
 
         def all(self):
             self.load()
+            r = lax.dot_general(
+                W[...].reshape(1536, 2304), self.ogs, (((1,), (1,)), ((), ())),
+                preferred_element_type=F32,
+            )
+            for j in range(self.n):
+                PT[self.t + j] = r[:, j * 128 : (j + 1) * 128].reshape(2, 4, 192, 128)
             self.far()
-            self.near_p()
-            self.near_m()
-            self.part(3)
+            self.near()
 
         def mid(self):
             self.g1.wait()
@@ -170,18 +169,16 @@
         def out(self):
             self.z.wait()
             for t in range(self.t, self.t + self.n):
-                FN[t] = FN[t] + RZ[t]
-                local(FN.at[t], ig_out.at[order[t]])
-
-    def wg(H, first, last):
+                at = pl.ds(pl.multiple_of(order[t] * 128, 128), 128)
+                ig_out[:, at] = (FN[t] + RZ[t]).astype(BF16)
+
+    def wg(H, first):
         for m in range(3):
             rows = pl.ds(m * 256, 256)
             a = ACT[H, :, :, :, :, rows].reshape(512, 256)
             g = OG[H].reshape(512, 1152)
             d = lax.dot_general(a, g, (((0,), (0,)), ((), ())), preferred_element_type=F32)
             ACC[rows] = d if first else ACC[rows] + d
-            if last:
-                local(ACC.at[rows], wg_out.at[rows])
 
     def again(group, H, X, half, dev):
         group.send(OG.at[H, X, half], OG.at[H, X, half], dev)
@@ -192,18 +189,19 @@
     c_og0.wait()
     s0.load()
     d_w[0].wait()
+    s0.part(0)
     s0.far()
-    d_w[1].wait()
-    s0.near_p()
     x0a.wait()
     again(x0ef, h, xm, HA, to_xp)
+    d_w[1].wait()
+    d_w[2].wait()
+    s0.part(1)
+    s0.part(2)
+    s0.near()
     x0b.wait()
     again(x0ef, h, xp, HB, to_xm)
-    d_w[2].wait()
-    s0.near_m()
-    d_w[3].wait()
-    s0.part(3)
     s0.mid()
+
     c_og12 = Group(OGP.at[pl.ds(1, 2)])
     x0cd.wait()
     c_og12.send(OG.at[h, xm], OGP.at[1], to_core)
@@ -218,23 +216,31 @@
     again(b_in, hp, x, HB, to_xp)
     again(z2ab, hm, x, HA, to_hp)
     again(z2ab, hp, x, HB, to_hm)
+    d_w[3].wait()
+    s0.part(3)
 
     c_og12.wait()
-    s1.all()
+    s1.load()
+    s1.part(0)
+    s1.far()
+    s1.part(1)
+    s1.part(2)
+    s1.near()
     x0ef.wait()
     c_og3 = send(OG.at[h, x2], OGP.at[3], to_core)
-    s0.end()
-    c_og3.wait()
-    s3.all()
+    s1.part(3)
     ab1.wait()
     again(a_in, hm, xm, HA, to_xp)
     again(b_in, hp, xp, HB, to_xm)
-    s1.mid()
     z0cd.wait()
     again(ab3, hm, x, HB, to_xm)
     again(ab3, hp, x, HA, to_xp)
     again(a_in, hm, x, HB, to_xp)
     again(b_in, hp, x, HA, to_xm)
+    s0.end()
+    c_og3.wait()
+    s3.all()
+    s1.mid()
     s3.mid()
 
     def act_y(i):
@@ -264,12 +270,14 @@
     l_act.wait()
     act_y(0)
     act_y(1)
+    act_y(2)
     c_own = send(ACT.at[:, :, y, k], ACT.at[:, :, y, k], to_core)
     ab3.wait()
     again(b_in, hp, xm, HA, to_xp)
     again(a_in, hm, xp, HB, to_xm)
     s0.out()
     s1.end()
+    act_in(0)
     e13, e_in = Group(two_halves), Group(OG.at[h, pl.ds(0, 2)])
     z2ab.wait()
     again(e13, h2, x, HA, to_xp)
@@ -277,49 +285,43 @@
     again(e_in, h2, x, HA, to_xm)
     again(e_in, h2, x, HB, to_xp)
     s3.end()
-    act_in(0)
-    act_y(2)
-    s1.out()
     act_in(1)
     act_y(3)
+    s1.out()
+    act_in(2)
     act_all(0)
-    s3.out()
     e13.wait()
     again(e_in, h2, xm, HA, to_xp)
     again(e_in, h2, xp, HB, to_xm)
     c_own.wait()
     c_act[0].wait()
-    wg(h, True, False)
-    act_in(2)
+    wg(h, True)
     act_all(1)
+    act_in(3)
+    s3.out()
     a_in.wait()
     c_act[1].wait()
-    wg(hm, False, False)
-    act_in(3)
+    wg(hm, False)
     act_all(2)
     b_in.wait()
     c_act[2].wait()
-    wg(hp, False, False)
     act_all(3)
+    wg(hp, False)
     e_in.wait()
     c_act[3].wait()
-    wg(h2, False, True)
-    for d in locs[3:]:
-        d.wait()
+    wg(h2, False)
     for d in started:
         d.wait_send()
 
 
 def body(activations, out_grad, weight):
-    any_ = pl.BlockSpec(memory_space=pl.ANY)
-    ig, wg = pl.pallas_call(
+    hbm = pl.BlockSpec(memory_space=pltpu.HBM)
+    vmem = pl.BlockSpec(memory_space=pltpu.VMEM)
+    input_grad, weight_grad = pl.pallas_call(
         kernel,
-        out_shape=(
-            jax.ShapeDtypeStruct((4, 192, 128), F32),
-            jax.ShapeDtypeStruct((768, 1152), F32),
-        ),
-        in_specs=[any_] * 3,
-        out_specs=(any_, any_),
+        out_shape=(pltpu.VMEM((192, 512), BF16), pltpu.VMEM((768, 1152), F32)),
+        in_specs=[hbm] * 3,
+        out_specs=(vmem, vmem),
         scratch_shapes=[
             pltpu.VMEM((2, 4, 192, 2304), BF16),
             pltpu.VMEM((4, 4, 128, 1152), BF16),
@@ -331,18 +333,16 @@
             pltpu.VMEM((4, 192, 128), F32),
             pltpu.VMEM((4, 192, 128), F32),
             pltpu.VMEM((4, 192, 128), F32),
-            pltpu.VMEM((768, 1152), F32),
             pltpu.SemaphoreType.DMA((SEMS,)),
             pltpu.SemaphoreType.DMA((SEMS,)),
-            pltpu.SemaphoreType.DMA((16,)),
+            pltpu.SemaphoreType.DMA((4,)),
         ],
         compiler_params=pltpu.CompilerParams(
-            collective_id=0, has_side_effects=True, vmem_limit_bytes=56 * 1024 * 1024
+            collective_id=0, has_side_effects=True, vmem_limit_bytes=48 * 1024 * 1024
         ),
         cost_estimate=pl.CostEstimate(flops=7_300_000_000, bytes_accessed=20_000_000, transcendentals=0),
-    )(activations, out_grad, weight.reshape(2, 4, 2, 192, 1152))
-    input_grad = jnp.transpose(ig, (0, 2, 1)).reshape(512, 192).astype(BF16)
-    return input_grad, wg.reshape(1, 1, 768, 1152)
+    )(*[pltpu.with_memory_space_constraint(v, pltpu.HBM) for v in (activations, out_grad, weight.reshape(2, 4, 2, 192, 1152))])
+    return input_grad.T, weight_grad.reshape(1, 1, 768, 1152)
 
 
 def solution(mesh):

time: 70.3 us -> 67.3 us (0.957)
  other arithmetic: 1.69 us -> 0 us
  local copies, waits for them, and re-layouts: 4.02 us -> 2.47 us
    convert_element_type x1 -> x0, other arithmetic: 1.69 us -> none  [body(): input_grad = jnp.transpose(ig, (0, 2, 1)).reshape(512, 192).astype(BF16)]
    unnamed x1 -> x2, local copies, waits for them, and re-layouts: 4.02 us -> 2.47 us
where the time goes in v3:
time: 67.3 us; the launch traced here: 67.2 us
  Pallas kernels  64.1 us (95%)
  local copies, waits for them, and re-layouts  2.47 us (4%)
    pallas_call x1, Pallas kernels, body(): pl.pallas_call(kernel, out_shape=(pltpu.VMEM((192, 512), BF16), pltpu.VME...  64.1 us
    unnamed x2, local copies, waits for them, and re-layouts  2.47 us

profile of v3, /device:TPU:1, one launch (start us, length us, event | category | flops | bytes accessed | tf_op | source)
XLA Modules:
  0.0 67.2 jit_solution(15045624919120072395)
XLA Ops:
  0.6 64.1 %shard_map.50 = (bf16[192,512]{1,0:T(8,128)(2,1)S(1)}, f32[768,1152]{1,0:T(8,128)S(1)}) custom-call(bf16[32,3072]{1,0:T(8,128)(2,1)} %act.1, bf16[128,1152]{1,0:T(8,128)(2,1)} %og.1, bf16[2,4,2,192,1152]{4,3,2,1,0:T(8,128)(2,1)} %bitcast.5), custom_call_target="tpu_custom_call" | custom-call | flops 7299999744 | bytes 20000000 | tf_op jit(solution)/shard_map/pallas_call | solution.py:320
  64.7 0.7 %copy.7 = bf16[512,192]{0,1:T(8,128)(2,1)} copy(bf16[512,192]{0,1:T(8,128)(2,1)S(1)} %bitcast.4) | data formatting | bytes 393216
  65.4 1.8 %copy.8 = f32[1,1,768,1152]{3,2,1,0:T(8,128)} copy(f32[1,1,768,1152]{3,2,1,0:T(8,128)S(1)} %bitcast.3) | data formatting | bytes 7077888

commit v4 on v3

--- a/solution.py
+++ b/solution.py
@@ -200,12 +200,15 @@
     s0.near()
     x0b.wait()
     again(x0ef, h, xp, HB, to_xm)
-    s0.mid()
-
     c_og12 = Group(OGP.at[pl.ds(1, 2)])
     x0cd.wait()
     c_og12.send(OG.at[h, xm], OGP.at[1], to_core)
     c_og12.send(OG.at[h, xp], OGP.at[2], to_core)
+    s0.mid()
+    c_og12.wait()
+    s1.load()
+    s1.part(0)
+    s1.far()
 
     ab1, ab3 = Group(two_halves), Group(two_halves)
     a_in, b_in = Group(OG.at[h, pl.ds(0, 2)]), Group(OG.at[h, pl.ds(0, 2)])
@@ -216,31 +219,26 @@
     again(b_in, hp, x, HB, to_xp)
     again(z2ab, hm, x, HA, to_hp)
     again(z2ab, hp, x, HB, to_hm)
-    d_w[3].wait()
-    s0.part(3)
-
-    c_og12.wait()
-    s1.load()
-    s1.part(0)
-    s1.far()
     s1.part(1)
     s1.part(2)
     s1.near()
     x0ef.wait()
     c_og3 = send(OG.at[h, x2], OGP.at[3], to_core)
+    d_w[3].wait()
+    s0.part(3)
     s1.part(3)
     ab1.wait()
     again(a_in, hm, xm, HA, to_xp)
     again(b_in, hp, xp, HB, to_xm)
+    s1.mid()
     z0cd.wait()
     again(ab3, hm, x, HB, to_xm)
     again(ab3, hp, x, HA, to_xp)
     again(a_in, hm, x, HB, to_xp)
     again(b_in, hp, x, HA, to_xm)
-    s0.end()
     c_og3.wait()
     s3.all()
-    s1.mid()
+    s0.end()
     s3.mid()
 
     def act_y(i):
@@ -277,22 +275,22 @@
     again(a_in, hm, xp, HB, to_xm)
     s0.out()
     s1.end()
-    act_in(0)
     e13, e_in = Group(two_halves), Group(OG.at[h, pl.ds(0, 2)])
     z2ab.wait()
     again(e13, h2, x, HA, to_xp)
     again(e13, h2, x, HB, to_xm)
     again(e_in, h2, x, HA, to_xm)
     again(e_in, h2, x, HB, to_xp)
+    act_in(0)
     s3.end()
     act_in(1)
     act_y(3)
     s1.out()
     act_in(2)
-    act_all(0)
     e13.wait()
     again(e_in, h2, xm, HA, to_xp)
     again(e_in, h2, xp, HB, to_xm)
+    act_all(0)
     c_own.wait()
     c_act[0].wait()
     wg(h, True)

time: 67.3 us -> 65.5 us (0.973)
  Pallas kernels: 64.1 us -> 62.3 us
    pallas_call x1, Pallas kernels: 64.1 us -> 62.3 us  [body(): pl.pallas_call(kernel, out_shape=(pltpu.VMEM((192, 512), BF16), pltpu.VME...]
where the time goes in v4:
time: 65.5 us; the launch traced here: 65.4 us
  Pallas kernels  62.3 us (95%)
  local copies, waits for them, and re-layouts  2.47 us (4%)
    pallas_call x1, Pallas kernels, body(): pl.pallas_call(kernel, out_shape=(pltpu.VMEM((192, 512), BF16), pltpu.VME...  62.3 us
    unnamed x2, local copies, waits for them, and re-layouts  2.47 us

profile of v4, /device:TPU:1, one launch (start us, length us, event | category | flops | bytes accessed | tf_op | source)
XLA Modules:
  0.0 65.4 jit_solution(16053792880625152850)
XLA Ops:
  0.6 62.3 %shard_map.50 = (bf16[192,512]{1,0:T(8,128)(2,1)S(1)}, f32[768,1152]{1,0:T(8,128)S(1)}) custom-call(bf16[32,3072]{1,0:T(8,128)(2,1)} %act.1, bf16[128,1152]{1,0:T(8,128)(2,1)} %og.1, bf16[2,4,2,192,1152]{4,3,2,1,0:T(8,128)(2,1)} %bitcast.5), custom_call_target="tpu_custom_call" | custom-call | flops 7299999744 | bytes 20000000 | tf_op jit(solution)/shard_map/pallas_call | solution.py:318
  62.9 0.7 %copy.7 = bf16[512,192]{0,1:T(8,128)(2,1)} copy(bf16[512,192]{0,1:T(8,128)(2,1)S(1)} %bitcast.4) | data formatting | bytes 393216
  63.6 1.8 %copy.8 = f32[1,1,768,1152]{3,2,1,0:T(8,128)} copy(f32[1,1,768,1152]{3,2,1,0:T(8,128)S(1)} %bitcast.3) | data formatting | bytes 7077888
